TPU v7x, 32 devices: a whole 2x2x4 slice. The times are simulated.
32 devices in a mesh: groups: 2 (over y), tile: 4 (over x, core), cuts: 4 (over z).
Axes of the slice: x: 2, y: 2, z: 4, core: 2. Of those that a mesh axis runs over, the one named last changes fastest.
Arguments:
- trade: bfloat16 [16, 4, 256, 8192], P(('groups', 'cuts'), 'tile'), parts along dimension 0, may hold values from -6 to 6
- factor: bfloat16 [32768, 256], P(('groups', 'tile', 'cuts')), parts along dimension 0, may hold values from -0.375 to 0.375
- scales: float32 [16, 256], P(('groups', 'cuts')), parts along dimension 0, may hold values from 0.1 to 1.9
- core: float32 [512, 256], P('groups'), parts along dimension 0, may hold values from -4 to 4
Outputs:
- grad_factor: float32 [32768, 256], P(('groups', 'tile', 'cuts')), parts along dimension 0
- grad_window: float32 [1024, 256], P(('groups', 'cuts')), parts along dimension 0
- grad_core: float32 [512, 256], P('groups'), parts along dimension 0
- grad_scales: float32 [16, 256], P(('groups', 'cuts')), parts along dimension 0
There are 2 independent parts, one for each index of `groups`. A program takes and returns all parts, laid end to end along the dimension named above; each array names one. Nothing has to cross between parts.
All inputs are finite; a program needn't handle non-finite values.
Results may differ from a plain program's by a relative error of at most 0.00055.
Values may be sent and summed in bfloat16 or wider, within the bound.
A program may use at most 128 MiB of HBM per device.

v0:
```python
import math
import jax
import jax.numpy as jnp
from jax import lax
from jax.sharding import PartitionSpec as P

P_SIZE = 256


def swapped(value, axis, distance):
    mask = 2**distance
    pairs = [(source, source ^ mask) for source in range(lax.axis_size(axis))]
    return lax.ppermute(value, axis, pairs)


def from_root(block, axis, source):
    block = jnp.where(lax.axis_index(axis) == source, block, jnp.zeros_like(block))
    return lax.psum(block, axis)


def body(trade, factor, scales, core):
    n_cuts = lax.axis_size("cuts")
    band_index = lax.axis_index("tile") % 2
    months = trade.shape[0]
    rows_band = trade.shape[2]
    window_size = 2 * rows_band
    highest = lax.Precision.HIGHEST
    own_block = lax.all_gather(factor, "cuts", axis=0, tiled=True)
    block = own_block.shape[0]
    partner_block = swapped(own_block, "tile", 0)
    first_block = jnp.where(band_index == 0, own_block, partner_block)
    second_block = jnp.where(band_index == 0, partner_block, own_block)
    column_factor = jnp.concatenate([first_block, second_block], 0)
    window_block = from_root(own_block, "tile", 0)
    window_rows = lax.dynamic_slice_in_dim(window_block, band_index * rows_band, rows_band, 0)
    window32 = window_rows.astype(jnp.float32)
    coef = 1.0 / math.sqrt(months * n_cuts * window_size)
    acc_columns = jnp.zeros((2 * block, P_SIZE), jnp.float32)
    acc_window = jnp.zeros((rows_band, P_SIZE), jnp.float32)
    acc_core = jnp.zeros((P_SIZE, P_SIZE), jnp.float32)
    diag_terms = []
    for month in range(months):
        diag_k = scales[month]
        inner = diag_k[:, None] * core * diag_k[None, :]
        mapped = jnp.dot(window32, inner, precision=highest).astype(jnp.bfloat16)
        model = lax.dot_general(
            mapped, column_factor, (((1,), (1,)), ((), ())), preferred_element_type=jnp.float32
        )
        residual = (trade[month, 0].astype(jnp.float32) - model).astype(jnp.bfloat16)
        acc_columns = acc_columns + lax.dot_general(
            residual, mapped, (((0,), (0,)), ((), ())), preferred_element_type=jnp.float32
        )
        projected = jnp.dot(residual, column_factor, preferred_element_type=jnp.float32)
        acc_window = acc_window + jnp.dot(projected, inner.T, precision=highest)
        gram = jnp.dot(window32.T, projected, precision=highest)
        acc_core = acc_core + diag_k[:, None] * gram * diag_k[None, :]
        weighted = gram * core
        diag_terms.append(
            jnp.dot(weighted, diag_k, precision=highest)
            + jnp.dot(weighted.T, diag_k, precision=highest)
        )
    diag_stack = jnp.stack(diag_terms, 0)
    halves = acc_columns.reshape(2, block, P_SIZE)
    mine = jnp.where(band_index == 0, halves[0], halves[1])
    other = jnp.where(band_index == 0, halves[1], halves[0])
    received = swapped(other, "tile", 0)
    grad_factor = lax.psum_scatter(mine + received, "cuts", scatter_dimension=0, tiled=True)
    padded = lax.dynamic_update_slice_in_dim(
        jnp.zeros((window_size, P_SIZE), jnp.float32), acc_window, band_index * rows_band, 0
    )
    window_part = lax.psum_scatter(padded, "cuts", scatter_dimension=0, tiled=True)
    window_total = lax.psum(window_part, "tile")
    core_total = lax.psum(acc_core, ("tile", "cuts"))
    diag_total = lax.psum(diag_stack, "tile")
    return (-coef * grad_factor, -coef * window_total, -coef * core_total, -coef * diag_total)


def solution(mesh):
    return jax.shard_map(
        body,
        mesh=mesh,
        in_specs=(
            P(("groups", "cuts"), "tile", None, None),
            P(("groups", "tile", "cuts"), None),
            P(("groups", "cuts"), None),
            P("groups", None),
        ),
        out_specs=(
            P(("groups", "tile", "cuts"), None),
            P(("groups", "cuts"), None),
            P("groups", None),
            P(("groups", "cuts"), None),
        ),
        check_vma=False,
    )
```

profile of v0, /device:TPU:0, one launch (start us, length us, event | category | flops | bytes accessed | tf_op | source)
XLA Modules:
  0.0 385.2 jit_solution(4281532647967686441)
XLA Ops:
  7.2 0.0 all-gather.2.cloned.1.call-start
  7.2 0.7 all-gather.2.cloned.1.call-update
  7.9 0.0 all-reduce.4.cloned.1.call-start
  7.9 50.3 %all-gather.2.cloned.1.call-done = bf16[4096,256]{1,0:T(8,128)(2,1)} async-done(((bf16[1024,256]{1,0:T(8,128)(2,1)}), bf16[4096,256]{1,0:T(8,128)(2,1)}) %all-gather.2.cloned.1.call-update) | async-done | bytes 2097168 | tf_op jit(solution)/shard_map/all_gather | solution.py:28
  58.2 0.0 collective-permute-start
  58.2 0.0 copy-start.8
  58.2 0.0 copy-start.1
  58.2 4.5 %collective-permute-done = bf16[4096,256]{1,0:T(8,128)(2,1)} collective-permute-done((bf16[4096,256]{1,0:T(8,128)(2,1)}, bf16[4096,256]{1,0:T(8,128)(2,1)}, u32[]{:S(2)}, u32[]{:S(2)}) %collective-permute-start) | collective-permute-done | bytes 2097184 | tf_op jit(solution)/shard_map/ppermute | solution.py:13
  62.7 4.6 %broadcast_select_fusion.2 = (bf16[4096,256]{1,0:T(8,128)(2,1)S(1)}, bf16[4096,256]{1,0:T(8,128)(2,1)}, bf16[4096,256]{1,0:T(8,128)(2,1)}) fusion(bf16[4096,256]{1,0:T(8,128)(2,1)} %all-gather.2.cloned.1.call-done, bf16[4096,256]{1,0:T(8,128)(2,1)} %collective-permute-done, pred[]{:T(512)S(6)} %eq.6, pred[]{:T(512)S(6)} %eq.12), kind=kLoop, calls=%fused_computation.10 | loop fusion | flops 3145728 | bytes 10485762 | tf_op jit(solution)/shard_map/jit(_where)/select_n | solution.py:31
  67.4 0.0 all-reduce.4.cloned.1.call-update
  67.4 0.0 reduce-scatter.5.cloned.1.call-start
  67.5 0.0 copy-done.8
  67.5 50.2 %all-reduce.4.cloned.1.call-done = bf16[4096,256]{1,0:T(8,128)(2,1)} async-done(((bf16[4096,256]{1,0:T(8,128)(2,1)}), bf16[4096,256]{1,0:T(8,128)(2,1)}) %all-reduce.4.cloned.1.call-update) | async-done | bytes 2097168 | tf_op jit(solution)/shard_map/psum | solution.py:18
  117.6 0.0 copy-done.1
  117.6 1.3 convolution_convert_fusion.1
  118.9 0.0 copy-start.6
  119.0 4.3 %fusion = bf16[256,8192]{1,0:T(8,128)(2,1)S(1)} fusion(bf16[256,256]{1,0:T(8,128)(2,1)S(1)} %convolution_convert_fusion.1, bf16[2,1,256,8192]{3,2,1,0:T(8,128)(2,1)} %param.4, bf16[4096,256]{1,0:T(8,128)(2,1)} %get-tuple-element.5, bf16[4096,256]{1,0:T(8,128)(2,1)S(1)} %get-tuple-element.4), kind=kOutput, calls=%fused_computation.3 | convolution fusion | flops 1088421888 | bytes 12713984 | tf_op jit(solution)/shard_map/dot_general | solution.py:46
  123.2 0.0 copy-start.4
  123.2 1.5 convolution_convert_fusion
  124.7 0.0 copy-done.6
  124.7 9.6 %fusion.1 = bf16[256,8192]{1,0:T(8,128)(2,1)S(1)} fusion(bf16[256,256]{1,0:T(8,128)(2,1)S(1)} %convolution_convert_fusion, bf16[2,1,256,8192]{3,2,1,0:T(8,128)(2,1)} %param.4, bf16[4096,256]{1,0:T(8,128)(2,1)S(1)} %copy-done.6, bf16[4096,256]{1,0:T(8,128)(2,1)S(1)} %get-tuple-element.4), kind=kOutput, calls=%fused_computation.4 | convolution fusion | flops 1088421888 | bytes 12713984 | tf_op jit(solution)/shard_map/dot_general | solution.py:46
  134.3 0.0 copy-done.4
  134.4 0.0 copy-start.2
  134.4 1.3 fusion.43
  135.7 0.6 copy-done.2
  136.3 1.3 convolution_add_fusion
  137.7 0.0 copy-start
  137.7 2.8 slice_select_fusion
  140.5 1.6 copy-done
  142.2 0.0 collective-permute-start.1
  142.2 0.0 copy-start.3
  142.2 0.0 copy-start.7
  142.2 4.2 %fusion.41 = f32[256,256]{1,0:T(8,128)S(1)} fusion(bf16[256,8192]{1,0:T(8,128)(2,1)} %copy-done.4, bf16[4096,256]{1,0:T(8,128)(2,1)} %get-tuple-element.5, bf16[4096,256]{1,0:T(8,128)(2,1)S(1)} %get-tuple-element.4), kind=kOutput, calls=%fused_computation.61 | convolution fusion | flops 1082130432 | bytes 8650752 | tf_op jit(solution)/shard_map/dot_general | solution.py:53
  146.4 0.5 fusion.7
  146.9 0.0 copy-done.3
  146.9 0.0 copy-done.7
  146.9 1.2 fusion.40
  148.2 0.5 fusion.2
  148.7 0.0 copy-start.5
  148.7 0.8 copy-done.5
  149.5 0.0 reduce-scatter.5.cloned.1.call-update
  149.5 0.0 all-reduce.8.cloned.1.call-start
  149.6 1.2 fusion.24
  150.8 1.9 multiply_add_fusion
  152.8 0.0 all-reduce.8.cloned.1.call-update
  152.8 0.0 all-reduce.6.cloned.1.call-start
  152.8 18.8 %reduce-scatter.5.cloned.1.call-done = f32[128,256]{1,0:T(8,128)} async-done(((f32[512,256]{1,0:T(8,128)}), f32[128,256]{1,0:T(8,128)}) %reduce-scatter.5.cloned.1.call-update) | async-done | bytes 131088 | tf_op jit(solution)/shard_map/reduce_scatter | solution.py:71
  171.6 0.0 all-reduce.6.cloned.1.call-update
  171.6 0.0 reduce-scatter.3.cloned.1.call-start
  171.6 0.0 collective-permute-done.1
  171.7 7.4 %select_add_fusion = f32[4096,256]{1,0:T(8,128)} fusion(f32[4096,256]{1,0:T(8,128)} %collective-permute-done.1, f32[8192,256]{1,0:T(8,128)} %copy-done, pred[]{:T(512)S(6)} %eq.6), kind=kLoop, calls=%fused_computation.6 | loop fusion | flops 2097152 | bytes 16777216 | tf_op jit(solution)/shard_map/add | solution.py:67
  179.1 0.0 reduce-scatter.3.cloned.1.call-update
  179.1 0.3 fusion.20
  179.4 0.3 fusion.5
  179.6 0.3 fusion.17
  179.9 0.3 fusion.3
  180.3 5.7 %psum.31 = f32[2,256]{1,0:T(2,128)S(1)} all-reduce(f32[2,256]{1,0:T(2,128)S(1)} %pad_maximum_fusion.1), channel_id=1, replica_groups=mesh['groups'=2,'tile'=4,'cuts'=4] {'tile'}, use_global_device_ids=true, to_apply=%region_5.6 | all-reduce | flops 512 | bytes 4096 | tf_op jit(solution)/shard_map/psum | solution.py:74
  185.9 0.6 broadcast_multiply_fusion.3
  186.5 76.4 %all-reduce.8.cloned.1.call-done = f32[256,256]{1,0:T(8,128)} async-done(((f32[256,256]{1,0:T(8,128)}), f32[256,256]{1,0:T(8,128)}) %all-reduce.8.cloned.1.call-update) | async-done | bytes 262160 | tf_op jit(solution)/shard_map/psum | solution.py:73
  262.9 1.7 broadcast_multiply_fusion.1
  264.6 32.5 %all-reduce.6.cloned.1.call-done = f32[128,256]{1,0:T(8,128)} async-done(((f32[128,256]{1,0:T(8,128)}), f32[128,256]{1,0:T(8,128)}) %all-reduce.6.cloned.1.call-update) | async-done | bytes 131088 | tf_op jit(solution)/shard_map/psum | solution.py:72
  297.1 1.6 broadcast_multiply_fusion.2
  298.7 77.4 %reduce-scatter.3.cloned.1.call-done = f32[1024,256]{1,0:T(8,128)} async-done(((f32[4096,256]{1,0:T(8,128)}), f32[1024,256]{1,0:T(8,128)}) %reduce-scatter.3.cloned.1.call-update) | async-done | bytes 1048592 | tf_op jit(solution)/shard_map/reduce_scatter | solution.py:67
  376.1 2.3 broadcast_multiply_fusion
  (5 shorter events, 0.1 us)
Async XLA Ops:
  7.2 51.1 %all-gather.2.cloned.1.call-start = ((), (), s32[]{:S(2)}) async-start(), calls=%async_computation.2 | async-start | bytes 2621440 | tf_op jit(solution)/shard_map/all_gather | solution.py:28
  7.9 109.7 %all-reduce.4.cloned.1.call-start = ((), (), s32[]{:S(2)}) async-start(), calls=%async_computation.3 | async-start | bytes 4194304 | tf_op jit(solution)/shard_map/psum | solution.py:18
  58.2 4.5 %collective-permute-start = (bf16[4096,256]{1,0:T(8,128)(2,1)}, bf16[4096,256]{1,0:T(8,128)(2,1)}, u32[]{:S(2)}, u32[]{:S(2)}) collective-permute-start(bf16[4096,256]{1,0:T(8,128)(2,1)} %all-gather.2.cloned.1.call-done), channel_id=1, source_target_pairs={{0,4},{4,0},{8,12},{12,8},{1,5},{5,1},{9,13},{13,9},{2,6},{6,2},{1... | collective-permute-start | bytes 6291464 | tf_op jit(solution)/shard_map/ppermute | solution.py:13
  58.2 9.2 %copy-start.8 = (f32[2,256]{1,0:T(2,128)S(1)}, f32[2,256]{1,0:T(2,128)}, u32[]{:S(2)}) copy-start(f32[2,256]{1,0:T(2,128)} %param.6) | copy-start | bytes 6148
  58.2 59.4 %copy-start.1 = (f32[256,256]{1,0:T(8,128)S(1)}, f32[256,256]{1,0:T(8,128)}, u32[]{:S(2)}) copy-start(f32[256,256]{1,0:T(8,128)} %param.7) | copy-start | bytes 786436
  67.4 104.2 %reduce-scatter.5.cloned.1.call-start = ((), (), s32[]{:S(2)}) async-start(), calls=%async_computation.5 | async-start | bytes 655360 | tf_op jit(solution)/shard_map/reduce_scatter | solution.py:71
  118.9 5.8 %copy-start.6 = (bf16[4096,256]{1,0:T(8,128)(2,1)S(1)}, bf16[4096,256]{1,0:T(8,128)(2,1)}, u32[]{:S(2)}) copy-start(bf16[4096,256]{1,0:T(8,128)(2,1)} %get-tuple-element.5) | copy-start | bytes 6291460
  123.2 11.1 %copy-start.4 = (bf16[256,8192]{1,0:T(8,128)(2,1)}, bf16[256,8192]{1,0:T(8,128)(2,1)S(1)}, u32[]{:S(2)}) copy-start(bf16[256,8192]{1,0:T(8,128)(2,1)S(1)} %fusion) | copy-start | bytes 12582916
  134.4 2.0 copy-start.2
  137.7 4.5 %copy-start = (f32[8192,256]{1,0:T(8,128)}, f32[8192,256]{1,0:T(8,128)S(1)}, u32[]{:S(2)}) copy-start(f32[8192,256]{1,0:T(8,128)S(1)} %convolution_add_fusion) | copy-start | bytes 25165828
  142.2 29.5 %collective-permute-start.1 = (f32[4096,256]{1,0:T(8,128)}, f32[4096,256]{1,0:T(8,128)}, u32[]{:S(2)}, u32[]{:S(2)}) collective-permute-start(f32[4096,256]{1,0:T(8,128)} %slice_select_fusion), channel_id=1, source_target_pairs={{0,4},{4,0},{8,12},{12,8},{1,5},{5,1},{9,13},{13,9},{2,6},{6,2},{1... | collective-permute-start | bytes 12582920 | tf_op jit(solution)/shard_map/ppermute | solution.py:13
  142.2 4.7 %copy-start.3 = (bf16[256,8192]{1,0:T(8,128)(2,1)S(1)}, bf16[256,8192]{1,0:T(8,128)(2,1)}, u32[]{:S(2)}) copy-start(bf16[256,8192]{1,0:T(8,128)(2,1)} %copy-done.2) | copy-start | bytes 12582916
  142.2 4.8 %copy-start.7 = (bf16[4096,256]{1,0:T(8,128)(2,1)S(1)}, bf16[4096,256]{1,0:T(8,128)(2,1)}, u32[]{:S(2)}) copy-start(bf16[4096,256]{1,0:T(8,128)(2,1)} %get-tuple-element.5) | copy-start | bytes 6291460
  148.7 0.8 copy-start.5
  149.5 113.4 %all-reduce.8.cloned.1.call-start = ((), (), s32[]{:S(2)}) async-start(), calls=%async_computation.7 | async-start | bytes 524288 | tf_op jit(solution)/shard_map/psum | solution.py:73
  152.8 144.3 %all-reduce.6.cloned.1.call-start = ((), (), s32[]{:S(2)}) async-start(), calls=%async_computation.6 | async-start | bytes 262144 | tf_op jit(solution)/shard_map/psum | solution.py:72
  171.6 204.5 %reduce-scatter.3.cloned.1.call-start = ((), (), s32[]{:S(2)}) async-start(), calls=%async_computation.4 | async-start | bytes 5242880 | tf_op jit(solution)/shard_map/reduce_scatter | solution.py:67
Sparse Core Ops, SparseCore 0:
  9.6 48.6 all-gather.1
  67.5 50.0 all-reduce.3
  149.7 21.8 reduce-scatter.4
  175.8 87.1 all-reduce.7
  265.2 31.8 all-reduce.5
  299.3 76.7 reduce-scatter.2
where the time goes:
time: 385 us
  waiting for transfers between devices  311 us (81%)
  matrix products  30 us (8%)
  other arithmetic  21 us (5%)
  between operations  14.3 us (4%)
  blocking collectives  5.67 us (1%)
    reduce_scatter x1, waiting for transfers between devices, body(): lax.psum_scatter(mine + received, 'cuts', scatter_dimension=0, tiled=True)  77.4 us
    psum x1, waiting for transfers between devices, body(): core_total = lax.psum(acc_core, ('tile', 'cuts'))  76.4 us
    all_gather x1, waiting for transfers between devices, body(): own_block = lax.all_gather(factor, 'cuts', axis=0, tiled=True)  50.3 us
    psum x1, waiting for transfers between devices, from_root(): return lax.psum(block, axis)  50.2 us
    psum x1, waiting for transfers between devices, body(): window_total = lax.psum(window_part, 'tile')  32.5 us
    reduce_scatter x1, waiting for transfers between devices, body(): lax.psum_scatter(padded, 'cuts', scatter_dimension=0, tiled=True)  18.8 us
    dot_general x2, matrix products, body(): lax.dot_general(mapped, column_factor, (((1,), (1,)), ((), ())), preferre...  13.9 us
  transfers between devices with their start and end apart: 8, of which 7 were waited for; matrix products, arithmetic and copies ran while one was open for 6% of the time, Pallas kernels for 0%

commit v1 on v0

--- a/solution.py
+++ b/solution.py
@@ -70,7 +70,9 @@
     )
     window_part = lax.psum_scatter(padded, "cuts", scatter_dimension=0, tiled=True)
     window_total = lax.psum(window_part, "tile")
-    core_total = lax.psum(acc_core, ("tile", "cuts"))
+    core_total = acc_core
+    for mesh_axis in ("cuts", "tile"):
+        core_total = lax.psum(core_total, mesh_axis)
     diag_total = lax.psum(diag_stack, "tile")
     return (-coef * grad_factor, -coef * window_total, -coef * core_total, -coef * diag_total)
 

time: 385 us -> 332 us (0.86)
  waiting for transfers between devices: 311 us -> 258 us
    psum x1, waiting for transfers between devices: 76.4 us -> 33.6 us  [body(): core_total = lax.psum(core_total, mesh_axis)]
    psum x1, waiting for transfers between devices: 32.5 us -> 18.3 us  [body(): window_total = lax.psum(window_part, 'tile')]
    reduce_scatter x1, waiting for transfers between devices: 18.8 us -> 24.1 us  [body(): lax.psum_scatter(padded, 'cuts', scatter_dimension=0, tiled=True)]
  transfers between devices with their start and end apart: 8 -> 8, of which waited for: 7 -> 7; matrix products, arithmetic and copies ran while one was open for 6% -> 7% of each run, Pallas kernels for 0% -> 0%
where the time goes in v1:
time: 332 us
  waiting for transfers between devices  258 us (78%)
  matrix products  29.8 us (9%)
  other arithmetic  21 us (6%)
  between operations  14.3 us (4%)
  blocking collectives  5.68 us (2%)
    reduce_scatter x1, waiting for transfers between devices, body(): lax.psum_scatter(mine + received, 'cuts', scatter_dimension=0, tiled=True)  75.8 us
    all_gather x1, waiting for transfers between devices, body(): own_block = lax.all_gather(factor, 'cuts', axis=0, tiled=True)  50.3 us
    psum x1, waiting for transfers between devices, from_root(): return lax.psum(block, axis)  50.2 us
    psum x1, waiting for transfers between devices, body(): core_total = lax.psum(core_total, mesh_axis)  33.6 us
    reduce_scatter x1, waiting for transfers between devices, body(): lax.psum_scatter(padded, 'cuts', scatter_dimension=0, tiled=True)  24.1 us
    psum x1, waiting for transfers between devices, body(): window_total = lax.psum(window_part, 'tile')  18.3 us
    dot_general x2, matrix products, body(): lax.dot_general(mapped, column_factor, (((1,), (1,)), ((), ())), preferre...  13.7 us
    add x1, other arithmetic, body(): mine + received  7.4 us
  transfers between devices with their start and end apart: 8, of which 7 were waited for; matrix products, arithmetic and copies ran while one was open for 7% of the time, Pallas kernels for 0%

profile of v1, /device:TPU:0, one launch (start us, length us, event | category | flops | bytes accessed | tf_op | source)
XLA Modules:
  0.0 332.0 jit_solution(6907211747240615153)
XLA Ops:
  7.2 0.0 all-gather.2.cloned.1.call-start
  7.2 0.7 all-gather.2.cloned.1.call-update
  7.9 0.0 all-reduce.5.cloned.1.call-start
  7.9 50.3 %all-gather.2.cloned.1.call-done = bf16[4096,256]{1,0:T(8,128)(2,1)} async-done(((bf16[1024,256]{1,0:T(8,128)(2,1)}), bf16[4096,256]{1,0:T(8,128)(2,1)}) %all-gather.2.cloned.1.call-update) | async-done | bytes 2097168 | tf_op jit(solution)/shard_map/all_gather | solution.py:28
  58.2 0.0 collective-permute-start
  58.2 0.0 copy-start.8
  58.2 0.0 copy-start.1
  58.2 4.5 %collective-permute-done = bf16[4096,256]{1,0:T(8,128)(2,1)} collective-permute-done((bf16[4096,256]{1,0:T(8,128)(2,1)}, bf16[4096,256]{1,0:T(8,128)(2,1)}, u32[]{:S(2)}, u32[]{:S(2)}) %collective-permute-start) | collective-permute-done | bytes 2097184 | tf_op jit(solution)/shard_map/ppermute | solution.py:13
  62.7 4.6 %broadcast_select_fusion.2 = (bf16[4096,256]{1,0:T(8,128)(2,1)S(1)}, bf16[4096,256]{1,0:T(8,128)(2,1)}, bf16[4096,256]{1,0:T(8,128)(2,1)}) fusion(bf16[4096,256]{1,0:T(8,128)(2,1)} %all-gather.2.cloned.1.call-done, bf16[4096,256]{1,0:T(8,128)(2,1)} %collective-permute-done, pred[]{:T(512)S(6)} %eq.6, pred[]{:T(512)S(6)} %eq.12), kind=kLoop, calls=%fused_computation.10 | loop fusion | flops 3145728 | bytes 10485762 | tf_op jit(solution)/shard_map/jit(_where)/select_n | solution.py:31
  67.4 0.0 all-reduce.5.cloned.1.call-update
  67.4 0.0 all-reduce.7.cloned.1.call-start
  67.5 0.0 copy-done.8
  67.5 50.2 %all-reduce.5.cloned.1.call-done = bf16[4096,256]{1,0:T(8,128)(2,1)} async-done(((bf16[4096,256]{1,0:T(8,128)(2,1)}), bf16[4096,256]{1,0:T(8,128)(2,1)}) %all-reduce.5.cloned.1.call-update) | async-done | bytes 2097168 | tf_op jit(solution)/shard_map/psum | solution.py:18
  117.7 0.0 copy-done.1
  117.7 1.3 convolution_convert_fusion.1
  119.0 0.0 copy-start.6
  119.0 4.3 %fusion = bf16[256,8192]{1,0:T(8,128)(2,1)S(1)} fusion(bf16[256,256]{1,0:T(8,128)(2,1)S(1)} %convolution_convert_fusion.1, bf16[2,1,256,8192]{3,2,1,0:T(8,128)(2,1)} %param.4, bf16[4096,256]{1,0:T(8,128)(2,1)} %get-tuple-element.7, bf16[4096,256]{1,0:T(8,128)(2,1)S(1)} %get-tuple-element.6), kind=kOutput, calls=%fused_computation.3 | convolution fusion | flops 1088421888 | bytes 12713984 | tf_op jit(solution)/shard_map/dot_general | solution.py:46
  123.2 0.0 copy-start.4
  123.2 1.5 convolution_convert_fusion
  124.7 0.0 copy-done.6
  124.7 9.4 %fusion.1 = bf16[256,8192]{1,0:T(8,128)(2,1)S(1)} fusion(bf16[256,256]{1,0:T(8,128)(2,1)S(1)} %convolution_convert_fusion, bf16[2,1,256,8192]{3,2,1,0:T(8,128)(2,1)} %param.4, bf16[4096,256]{1,0:T(8,128)(2,1)S(1)} %copy-done.6, bf16[4096,256]{1,0:T(8,128)(2,1)S(1)} %get-tuple-element.6), kind=kOutput, calls=%fused_computation.4 | convolution fusion | flops 1088421888 | bytes 12713984 | tf_op jit(solution)/shard_map/dot_general | solution.py:46
  134.2 0.0 copy-done.4
  134.2 0.0 copy-start.2
  134.2 1.3 fusion.43
  135.5 0.7 copy-done.2
  136.2 1.3 convolution_add_fusion
  137.5 0.0 copy-start
  137.5 2.8 slice_select_fusion
  140.3 1.7 copy-done
  142.0 0.0 collective-permute-start.1
  142.0 0.0 copy-start.3
  142.0 0.0 copy-start.7
  142.0 4.2 %fusion.41 = f32[256,256]{1,0:T(8,128)S(1)} fusion(bf16[256,8192]{1,0:T(8,128)(2,1)} %copy-done.4, bf16[4096,256]{1,0:T(8,128)(2,1)} %get-tuple-element.7, bf16[4096,256]{1,0:T(8,128)(2,1)S(1)} %get-tuple-element.6), kind=kOutput, calls=%fused_computation.61 | convolution fusion | flops 1082130432 | bytes 8650752 | tf_op jit(solution)/shard_map/dot_general | solution.py:53
  146.2 1.2 fusion.24
  147.5 0.0 copy-done.3
  147.5 0.0 copy-done.7
  147.5 1.2 fusion.40
  148.7 1.9 multiply_add_fusion
  150.7 0.0 all-reduce.7.cloned.1.call-update
  150.7 0.2 reduce-scatter.5.cloned.1.call-start
  150.9 0.5 fusion.7
  151.5 0.5 fusion.2
  152.0 0.0 copy-start.5
  152.0 0.8 copy-done.5
  152.8 0.0 reduce-scatter.5.cloned.1.call-update
  152.8 0.0 all-reduce.9.cloned.1.call-start
  152.8 33.6 %all-reduce.7.cloned.1.call-done = f32[256,256]{1,0:T(8,128)} async-done(((f32[256,256]{1,0:T(8,128)}), f32[256,256]{1,0:T(8,128)}) %all-reduce.7.cloned.1.call-update) | async-done | bytes 262160 | tf_op jit(solution)/shard_map/psum | solution.py:75
  186.4 24.1 %reduce-scatter.5.cloned.1.call-done = f32[128,256]{1,0:T(8,128)} async-done(((f32[512,256]{1,0:T(8,128)}), f32[128,256]{1,0:T(8,128)}) %reduce-scatter.5.cloned.1.call-update) | async-done | bytes 131088 | tf_op jit(solution)/shard_map/reduce_scatter | solution.py:71
  210.5 0.0 all-reduce.9.cloned.1.call-update
  210.6 0.0 reduce-scatter.3.cloned.1.call-start
  210.6 0.0 collective-permute-done.1
  210.6 7.4 %select_add_fusion = f32[4096,256]{1,0:T(8,128)} fusion(f32[4096,256]{1,0:T(8,128)} %collective-permute-done.1, f32[8192,256]{1,0:T(8,128)} %copy-done, pred[]{:T(512)S(6)} %eq.6), kind=kLoop, calls=%fused_computation.6 | loop fusion | flops 2097152 | bytes 16777216 | tf_op jit(solution)/shard_map/add | solution.py:67
  218.0 0.0 reduce-scatter.3.cloned.1.call-update
  218.0 0.3 fusion.20
  218.3 0.3 fusion.5
  218.6 0.3 fusion.17
  218.9 0.3 fusion.3
  219.2 5.7 %psum.39 = f32[2,256]{1,0:T(2,128)S(1)} all-reduce(f32[2,256]{1,0:T(2,128)S(1)} %pad_maximum_fusion.1), channel_id=1, replica_groups=mesh['groups'=2,'tile'=4,'cuts'=4] {'tile'}, use_global_device_ids=true, to_apply=%region_6.7 | all-reduce | flops 512 | bytes 4096 | tf_op jit(solution)/shard_map/psum | solution.py:76
  224.9 0.6 broadcast_multiply_fusion.3
  225.5 18.3 %all-reduce.9.cloned.1.call-done = (f32[128,256]{1,0:T(8,128)}, f32[256,256]{1,0:T(8,128)}) async-done(((f32[128,256]{1,0:T(8,128)}, f32[256,256]{1,0:T(8,128)}), (f32[128,256]{1,0:T(8,128)}, f32[256,256]{1,0:T(8,128)})) %all-reduce.9.cloned.1.call-update) | async-done | bytes 393232 | tf_op jit(solution)/shard_map/psum | solution.py:72
  243.8 1.6 broadcast_multiply_fusion.2
  245.4 1.7 broadcast_multiply_fusion.1
  247.1 75.8 %reduce-scatter.3.cloned.1.call-done = f32[1024,256]{1,0:T(8,128)} async-done(((f32[4096,256]{1,0:T(8,128)}), f32[1024,256]{1,0:T(8,128)}) %reduce-scatter.3.cloned.1.call-update) | async-done | bytes 1048592 | tf_op jit(solution)/shard_map/reduce_scatter | solution.py:67
  322.9 2.3 broadcast_multiply_fusion
  (5 shorter events, 0.1 us)
Async XLA Ops:
  7.2 51.1 %all-gather.2.cloned.1.call-start = ((), (), s32[]{:S(2)}) async-start(), calls=%async_computation.2 | async-start | bytes 2621440 | tf_op jit(solution)/shard_map/all_gather | solution.py:28
  7.9 109.8 %all-reduce.5.cloned.1.call-start = ((), (), s32[]{:S(2)}) async-start(), calls=%async_computation.3 | async-start | bytes 4194304 | tf_op jit(solution)/shard_map/psum | solution.py:18
  58.2 4.5 %collective-permute-start = (bf16[4096,256]{1,0:T(8,128)(2,1)}, bf16[4096,256]{1,0:T(8,128)(2,1)}, u32[]{:S(2)}, u32[]{:S(2)}) collective-permute-start(bf16[4096,256]{1,0:T(8,128)(2,1)} %all-gather.2.cloned.1.call-done), channel_id=1, source_target_pairs={{0,4},{4,0},{8,12},{12,8},{1,5},{5,1},{9,13},{13,9},{2,6},{6,2},{1... | collective-permute-start | bytes 6291464 | tf_op jit(solution)/shard_map/ppermute | solution.py:13
  58.2 9.2 %copy-start.8 = (f32[2,256]{1,0:T(2,128)S(1)}, f32[2,256]{1,0:T(2,128)}, u32[]{:S(2)}) copy-start(f32[2,256]{1,0:T(2,128)} %param.6) | copy-start | bytes 6148
  58.2 59.4 %copy-start.1 = (f32[256,256]{1,0:T(8,128)S(1)}, f32[256,256]{1,0:T(8,128)}, u32[]{:S(2)}) copy-start(f32[256,256]{1,0:T(8,128)} %param.7) | copy-start | bytes 786436
  67.4 119.0 %all-reduce.7.cloned.1.call-start = ((), (), s32[]{:S(2)}) async-start(), calls=%async_computation.6 | async-start | bytes 524288 | tf_op jit(solution)/shard_map/psum | solution.py:75
  119.0 5.8 %copy-start.6 = (bf16[4096,256]{1,0:T(8,128)(2,1)S(1)}, bf16[4096,256]{1,0:T(8,128)(2,1)}, u32[]{:S(2)}) copy-start(bf16[4096,256]{1,0:T(8,128)(2,1)} %get-tuple-element.7) | copy-start | bytes 6291460
  123.2 10.9 %copy-start.4 = (bf16[256,8192]{1,0:T(8,128)(2,1)}, bf16[256,8192]{1,0:T(8,128)(2,1)S(1)}, u32[]{:S(2)}) copy-start(bf16[256,8192]{1,0:T(8,128)(2,1)S(1)} %fusion) | copy-start | bytes 12582916
  134.2 2.0 copy-start.2
  137.5 4.5 %copy-start = (f32[8192,256]{1,0:T(8,128)}, f32[8192,256]{1,0:T(8,128)S(1)}, u32[]{:S(2)}) copy-start(f32[8192,256]{1,0:T(8,128)S(1)} %convolution_add_fusion) | copy-start | bytes 25165828
  142.0 68.6 %collective-permute-start.1 = (f32[4096,256]{1,0:T(8,128)}, f32[4096,256]{1,0:T(8,128)}, u32[]{:S(2)}, u32[]{:S(2)}) collective-permute-start(f32[4096,256]{1,0:T(8,128)} %slice_select_fusion), channel_id=1, source_target_pairs={{0,4},{4,0},{8,12},{12,8},{1,5},{5,1},{9,13},{13,9},{2,6},{6,2},{1... | collective-permute-start | bytes 12582920 | tf_op jit(solution)/shard_map/ppermute | solution.py:13
  142.0 5.5 %copy-start.3 = (bf16[256,8192]{1,0:T(8,128)(2,1)S(1)}, bf16[256,8192]{1,0:T(8,128)(2,1)}, u32[]{:S(2)}) copy-start(bf16[256,8192]{1,0:T(8,128)(2,1)} %copy-done.2) | copy-start | bytes 12582916
  142.0 5.5 %copy-start.7 = (bf16[4096,256]{1,0:T(8,128)(2,1)S(1)}, bf16[4096,256]{1,0:T(8,128)(2,1)}, u32[]{:S(2)}) copy-start(bf16[4096,256]{1,0:T(8,128)(2,1)} %get-tuple-element.7) | copy-start | bytes 6291460
  150.7 59.8 %reduce-scatter.5.cloned.1.call-start = ((), (), s32[]{:S(2)}) async-start(), calls=%async_computation.5 | async-start | bytes 655360 | tf_op jit(solution)/shard_map/reduce_scatter | solution.py:71
  152.0 0.8 copy-start.5
  152.8 91.0 %all-reduce.9.cloned.1.call-start = ((), (), s32[]{:S(2)}) async-start(), calls=%async_computation.7 | async-start | bytes 786432 | tf_op jit(solution)/shard_map/psum | solution.py:72
  210.6 112.3 %reduce-scatter.3.cloned.1.call-start = ((), (), s32[]{:S(2)}) async-start(), calls=%async_computation.4 | async-start | bytes 5242880 | tf_op jit(solution)/shard_map/reduce_scatter | solution.py:67
Sparse Core Ops, SparseCore 0:
  9.6 48.6 all-gather.1
  67.5 50.0 all-reduce.4
  150.8 35.5 all-reduce.6
  189.1 21.3 reduce-scatter.4
  212.8 30.9 all-reduce.8
  246.1 76.7 reduce-scatter.2
